TPU v7x, 32 devices: a whole 2x2x4 slice. The times are simulated.
32 devices in a mesh: grp: 4 (over y, x), band: 8 (over z, core).
Axes of the slice: x: 2, y: 2, z: 4, core: 2. Of those that a mesh axis runs over, the one named last changes fastest.
Arguments:
- orbitals: bfloat16 [32, 64, 4096], P('band'), may hold values from -6 to 6
Outputs:
- exchange: float32 [32, 64, 4096], P('band', 'grp')
All inputs are finite; a program needn't handle non-finite values.
Results may differ from a plain program's by a relative error of at most 0.0003.
Values may be sent and summed in bfloat16 or wider, within the bound.
A program may use at most 128 MiB of HBM per device.

v0:
```python
import math

import jax
import jax.numpy as jnp
from jax import lax
from jax.sharding import PartitionSpec as P

ROUNDS = 2


CELL_LENGTH = 41.05
SCREENING = 0.106


def from_behind(shard, axis, by):
    count = lax.axis_size(axis)
    return lax.ppermute(shard, axis, [(i, (i + by) % count) for i in range(count)])


def kernel_table(grid):
    wavenum = jnp.arange(grid, dtype=jnp.int32)
    wavenum = jnp.where(wavenum < grid // 2, wavenum, wavenum - grid).astype(jnp.float32) * (
        2.0 * math.pi / CELL_LENGTH
    )
    squared = (
        wavenum[:, None, None] ** 2 + wavenum[None, :, None] ** 2 + wavenum[None, None, :] ** 2
    )
    safe = jnp.where(squared > 0, squared, 1.0)
    screened = 4.0 * math.pi * (1.0 - jnp.exp(-safe / (4.0 * SCREENING * SCREENING))) / safe
    return jnp.where(squared > 0, screened, math.pi / (SCREENING * SCREENING))


def hartley_pass(values, hartley, block_table):
    values = jnp.einsum("xyc,cd->xyd", values, block_table, precision=lax.Precision.HIGHEST)
    values = jnp.einsum("xyc,yk->xkc", values, hartley, precision=lax.Precision.HIGHEST)
    return jnp.einsum("xyc,xk->kyc", values, hartley, precision=lax.Precision.HIGHEST)


def potentials_of(own_band, arrived, hartley, block_table, kernel_wide):
    visits, grid, plane = arrived.shape
    density = own_band.astype(jnp.float32)[None] * arrived.astype(jnp.float32)
    density = (
        density.reshape(visits, grid, grid, grid)
        .transpose(1, 2, 0, 3)
        .reshape(grid, grid, visits * grid)
    )
    spectrum = hartley_pass(density, hartley, block_table) * kernel_wide
    result = hartley_pass(spectrum, hartley, block_table) / float(grid**3)
    return (
        result.reshape(grid, grid, visits, grid).transpose(2, 0, 1, 3).reshape(visits, grid, plane)
    )


def body(orbitals):
    own_count, grid, plane = orbitals.shape
    groups = lax.axis_size("grp")
    split_count = groups // own_count
    visits = own_count // split_count
    group_index = lax.axis_index("grp")
    band_row = group_index // split_count
    visit_start = group_index % split_count * visits
    own_band = lax.dynamic_index_in_dim(orbitals, band_row, 0, keepdims=False)
    outgoing = lax.dynamic_slice_in_dim(orbitals, visit_start, visits, 0)
    indices = jnp.arange(grid, dtype=jnp.int32)
    angles = (indices[:, None] * indices[None, :] % grid).astype(jnp.float32) * (
        2.0 * math.pi / grid
    )
    hartley = jnp.cos(angles) + jnp.sin(angles)
    block_table = jnp.kron(jnp.eye(visits, dtype=jnp.float32), hartley)
    kernel_wide = jnp.tile(kernel_table(grid), (1, 1, visits))
    exchange_home = jnp.zeros((grid, plane), jnp.float32)
    returned_sum = jnp.zeros((visits, grid, plane), jnp.float32)
    for distance in range(1, ROUNDS + 1):
        arrived = from_behind(outgoing, "band", distance)
        potentials = potentials_of(own_band, arrived, hartley, block_table, kernel_wide)
        home_term = -0.25 * jnp.sum(arrived.astype(jnp.float32) * potentials, axis=0)
        home_term, potentials = (home_term, potentials)
        exchange_home = exchange_home + home_term
        back_terms = -0.25 * own_band.astype(jnp.float32)[None] * potentials
        returned_sum = returned_sum + from_behind(back_terms, "band", -distance)
    zeros = jnp.zeros((own_count, grid, plane), jnp.float32)
    buffer = lax.dynamic_update_slice(zeros, exchange_home[None], (band_row, 0, 0))
    buffer = buffer + lax.dynamic_update_slice(zeros, returned_sum, (visit_start, 0, 0))
    return lax.psum_scatter(buffer, "grp", scatter_dimension=1, tiled=True)


def solution(mesh):
    return jax.shard_map(
        body,
        mesh=mesh,
        in_specs=(P("band", None, None),),
        out_specs=P("band", "grp", None),
        check_vma=False,
    )
```

profile of v0, /device:TPU:1, one launch (start us, length us, event | category | flops | bytes accessed | tf_op | source)
XLA Modules:
  0.0 396.4 jit_solution(5523591807365991684)
XLA Ops:
  12.2 4.8 %tile.13 = f32[64,64,4,64]{3,2,1,0:T(4,128)} broadcast(f32[64,64,64]{2,1,0:T(8,128)S(1)} %fusion.18), dimensions={0,1,3} | broadcast | bytes 5242880 | tf_op jit(solution)/shard_map/tile | solution.py:70
  17.0 8.7 %tile.14 = f32[64,64,256]{2,1,0:T(8,128)} reshape(f32[64,64,4,64]{3,2,1,0:T(4,128)} %tile.13) | data formatting | bytes 8388608 | tf_op jit(solution)/shard_map/tile | solution.py:70
  27.9 26.5 %collective-permute-done = bf16[4,64,4096]{2,1,0:T(8,128)(2,1)} collective-permute-done((bf16[4,64,4096]{2,1,0:T(8,128)(2,1)}, bf16[4,64,4096]{2,1,0:T(8,128)(2,1)}, u32[]{:S(2)}, u32[]{:S(2)}) %collective-permute-start) | collective-permute-done | bytes 2097184 | tf_op jit(solution)/shard_map/ppermute | solution.py:17
  54.4 24.9 %collective-permute-done.2 = bf16[4,64,4096]{2,1,0:T(8,128)(2,1)} collective-permute-done((bf16[4,64,4096]{2,1,0:T(8,128)(2,1)}, bf16[4,64,4096]{2,1,0:T(8,128)(2,1)}, u32[]{:S(2)}, u32[]{:S(2)}) %collective-permute-start.2) | collective-permute-done | bytes 2097184 | tf_op jit(solution)/shard_map/ppermute | solution.py:17
  79.4 6.6 %convert_multiply_fusion.1 = (f32[4,64,4096]{2,1,0:T(8,128)}, f32[4,64,4096]{2,1,0:T(8,128)}) fusion(bf16[4,64,4096]{2,1,0:T(8,128)(2,1)} %collective-permute-done.2, f32[64,4096]{1,0:T(8,128)S(1)} %convert_bitcast_fusion, bf16[4,64,4096]{2,1,0:T(8,128)(2,1)} %collective-permute-done), kind=kLoop, calls=%fused_computation.3 | loop fusion | flops 4194304 | bytes 13631488 | tf_op jit(solution)/shard_map/mul | solution.py:41
  86.0 7.9 %reshape.182 = f32[4,64,64,64]{3,2,1,0:T(8,128)} reshape(f32[4,64,4096]{2,1,0:T(8,128)} %get-tuple-element.9) | data formatting | bytes 8388608 | tf_op jit(solution)/shard_map/reshape | solution.py:43
  93.9 14.6 %copy.42 = f32[4,64,64,64]{3,0,2,1:T(4,128)} copy(f32[4,64,64,64]{3,2,1,0:T(8,128)} %reshape.182) | data formatting | bytes 8388608 | tf_op jit(solution)/shard_map/reshape | solution.py:43
  108.4 8.9 %reshape.183 = f32[64,64,256]{2,1,0:T(8,128)} reshape(f32[64,64,4,64]{3,2,1,0:T(4,128)} %bitcast.67) | data formatting | bytes 8388608 | tf_op jit(solution)/shard_map/reshape | solution.py:45
  117.4 6.0 %fusion.86 = f32[64,64,256]{2,1,0:T(8,128)S(1)} fusion(f32[64,64,256]{2,1,0:T(8,128)} %reshape.183, f32[256,256,1]{1,0,2:T(8,128)S(1)} %reshape.186), kind=kOutput, calls=%fused_computation.105 | convolution fusion | flops 3221225472 | bytes 8650752 | tf_op jit(solution)/shard_map/xyc,cd->xyd/dot_general | solution.py:34
  127.4 6.0 %fusion.4 = f32[64,64,256]{2,0,1:T(8,128)S(1)} fusion(f32[64,64,256]{2,0,1:T(8,128)S(1)} %fusion.38), kind=kOutput, calls=%fused_computation.10 | convolution fusion | flops 805367808 | bytes 8388608 | tf_op jit(solution)/shard_map/xyc,xk->kyc/dot_general | solution.py:36
  133.5 5.7 %fusion.11 = f32[64,64,256]{2,1,0:T(8,128)S(1)} fusion(f32[256,256,1]{1,0,2:T(8,128)S(1)} %reshape.186, f32[64,64,256]{2,1,0:T(8,128)S(1)} %copy-done, f32[64,64,256]{2,0,1:T(8,128)S(1)} %fusion.4), kind=kOutput, calls=%fused_computation.18 | convolution fusion | flops 3222274048 | bytes 12845056 | tf_op jit(solution)/shard_map/xyc,cd->xyd/dot_general | solution.py:34
  139.2 4.1 %fusion.35 = f32[64,64,256]{2,0,1:T(8,128)S(1)} fusion(f32[64,64,256]{2,1,0:T(8,128)S(1)} %fusion.11), kind=kOutput, calls=%fused_computation.50 | convolution fusion | flops 805367808 | bytes 8388608 | tf_op jit(solution)/shard_map/xyc,yk->xkc/dot_general | solution.py:35
  143.3 7.0 %fusion.22 = f32[64,64,256]{2,0,1:T(8,128)} fusion(f32[64,64,256]{2,0,1:T(8,128)S(1)} %fusion.35), kind=kOutput, calls=%fused_computation.30 | convolution fusion | flops 806416384 | bytes 8388608 | tf_op jit(solution)/shard_map/xyc,xk->kyc/dot_general | solution.py:36
  150.4 8.2 %reshape.184 = f32[64,64,4,64]{3,2,0,1:T(4,128)} reshape(f32[64,64,256]{2,0,1:T(8,128)} %fusion.22) | data formatting | bytes 8388608 | tf_op jit(solution)/shard_map/reshape | solution.py:50
  158.6 11.5 %copy.9 = f32[4,64,64,64]{3,2,1,0:T(8,128)} copy(f32[4,64,64,64]{3,0,1,2:T(4,128)} %bitcast.68) | data formatting | bytes 8388608 | tf_op jit(solution)/shard_map/transpose | solution.py:50
  170.1 7.9 %reshape.185 = f32[4,64,4096]{2,1,0:T(8,128)} reshape(f32[4,64,64,64]{3,2,1,0:T(8,128)} %copy.9) | data formatting | bytes 8388608 | tf_op jit(solution)/shard_map/reshape | solution.py:50
  178.0 5.8 %fusion.1 = (f32[64,4096]{1,0:T(8,128)S(1)}, f32[4,64,4096]{2,1,0:T(8,128)}) fusion(f32[4,64,4096]{2,1,0:T(8,128)} %reshape.185, bf16[4,64,4096]{2,1,0:T(8,128)(2,1)} %collective-permute-done.2, f32[64,4096]{1,0:T(8,128)S(1)} %fusion.29), kind=kLoop, calls=%fused_computation.7 | loop fusion | flops 3932160 | bytes 12582912 | tf_op jit(solution)/shard_map/reduce_sum | solution.py:76
  185.8 8.3 %reshape.178 = f32[4,64,64,64]{3,2,1,0:T(8,128)} reshape(f32[4,64,4096]{2,1,0:T(8,128)} %get-tuple-element.10) | data formatting | bytes 8388608 | tf_op jit(solution)/shard_map/reshape | solution.py:43
  194.0 14.6 %copy.43 = f32[4,64,64,64]{3,0,2,1:T(4,128)} copy(f32[4,64,64,64]{3,2,1,0:T(8,128)} %reshape.178) | data formatting | bytes 8388608 | tf_op jit(solution)/shard_map/reshape | solution.py:43
  208.6 8.6 %reshape.179 = f32[64,64,256]{2,1,0:T(8,128)} reshape(f32[64,64,4,64]{3,2,1,0:T(4,128)} %bitcast.69) | data formatting | bytes 8388608 | tf_op jit(solution)/shard_map/reshape | solution.py:45
  217.2 6.2 %fusion.85 = f32[64,64,256]{2,1,0:T(8,128)S(1)} fusion(f32[64,64,256]{2,1,0:T(8,128)} %reshape.179, f32[256,256,1]{1,0,2:T(8,128)S(1)} %reshape.186), kind=kOutput, calls=%fused_computation.104 | convolution fusion | flops 3221225472 | bytes 8650752 | tf_op jit(solution)/shard_map/xyc,cd->xyd/dot_general | solution.py:34
  223.4 4.0 fusion.44
  227.4 6.0 %fusion.8 = f32[64,64,256]{2,0,1:T(8,128)S(1)} fusion(f32[64,64,256]{2,0,1:T(8,128)S(1)} %fusion.44), kind=kOutput, calls=%fused_computation.14 | convolution fusion | flops 805367808 | bytes 8388608 | tf_op jit(solution)/shard_map/xyc,xk->kyc/dot_general | solution.py:36
  233.4 5.7 %fusion.14 = f32[64,64,256]{2,1,0:T(8,128)S(1)} fusion(f32[256,256,1]{1,0,2:T(8,128)S(1)} %reshape.186, f32[64,64,256]{2,1,0:T(8,128)S(1)} %copy-done.1, f32[64,64,256]{2,0,1:T(8,128)S(1)} %fusion.8), kind=kOutput, calls=%fused_computation.22 | convolution fusion | flops 3222274048 | bytes 12845056 | tf_op jit(solution)/shard_map/xyc,cd->xyd/dot_general | solution.py:34
  239.2 4.1 %fusion.41 = f32[64,64,256]{2,0,1:T(8,128)S(1)} fusion(f32[64,64,256]{2,1,0:T(8,128)S(1)} %fusion.14), kind=kOutput, calls=%fused_computation.56 | convolution fusion | flops 805367808 | bytes 8388608 | tf_op jit(solution)/shard_map/xyc,yk->xkc/dot_general | solution.py:35
  243.3 7.1 %fusion.19 = f32[64,64,256]{2,0,1:T(8,128)} fusion(f32[64,64,256]{2,0,1:T(8,128)S(1)} %fusion.41), kind=kOutput, calls=%fused_computation.29 | convolution fusion | flops 806416384 | bytes 8388608 | tf_op jit(solution)/shard_map/xyc,xk->kyc/dot_general | solution.py:36
  250.4 8.3 %reshape.180 = f32[64,64,4,64]{3,2,0,1:T(4,128)} reshape(f32[64,64,256]{2,0,1:T(8,128)} %fusion.19) | data formatting | bytes 8388608 | tf_op jit(solution)/shard_map/reshape | solution.py:50
  258.7 11.5 %copy.7 = f32[4,64,64,64]{3,2,1,0:T(8,128)} copy(f32[4,64,64,64]{3,0,1,2:T(4,128)} %bitcast.70) | data formatting | bytes 8388608 | tf_op jit(solution)/shard_map/transpose | solution.py:50
  270.1 7.9 %reshape.181 = f32[4,64,4096]{2,1,0:T(8,128)} reshape(f32[4,64,64,64]{3,2,1,0:T(8,128)} %copy.7) | data formatting | bytes 8388608 | tf_op jit(solution)/shard_map/reshape | solution.py:50
  281.9 47.9 %collective-permute-done.1 = f32[4,64,4096]{2,1,0:T(8,128)S(1)} collective-permute-done((f32[4,64,4096]{2,1,0:T(8,128)S(1)}, f32[4,64,4096]{2,1,0:T(8,128)S(1)}, u32[]{:S(2)}, u32[]{:S(2)}) %collective-permute-start.1) | collective-permute-done | bytes 4194336 | tf_op jit(solution)/shard_map/ppermute | solution.py:17
  329.8 4.8 %add.165 = f32[4,64,4096]{2,1,0:T(8,128)} add(f32[4,64,4096]{2,1,0:T(8,128)S(1)} %collective-permute-done.1, f32[4,64,4096]{2,1,0:T(8,128)} %collective-permute-done.3) | non-fusion elementwise | flops 1048576 | bytes 12582912 | tf_op jit(solution)/shard_map/add | solution.py:80
  337.0 52.3 %reduce-scatter.2.cloned.1.call-done = f32[4,16,4096]{2,1,0:T(8,128)} async-done(((f32[4,64,4096]{2,1,0:T(8,128)}), f32[4,16,4096]{2,1,0:T(8,128)}) %reduce-scatter.2.cloned.1.call-update) | async-done | bytes 1048592 | tf_op jit(solution)/shard_map/reduce_scatter | solution.py:84
  (24 shorter events, 20.1 us)
Async XLA Ops:
  6.5 382.8 %reduce-scatter.2.cloned.1.call-start = ((), (), s32[]{:S(2)}) async-start(), calls=%async_computation.1 | async-start | bytes 5242880 | tf_op jit(solution)/shard_map/reduce_scatter | solution.py:84
  6.5 47.9 %collective-permute-start = (bf16[4,64,4096]{2,1,0:T(8,128)(2,1)}, bf16[4,64,4096]{2,1,0:T(8,128)(2,1)}, u32[]{:S(2)}, u32[]{:S(2)}) collective-permute-start(bf16[4,64,4096]{2,1,0:T(8,128)(2,1)} %param.1), channel_id=1, source_target_pairs={{0,1},{1,2},{2,3},{3,4},{4,5},{5,6},{6,7},{7,0},{8,9},{9,10},{10,1... | collective-permute-start | bytes 6291464 | tf_op jit(solution)/shard_map/ppermute | solution.py:17
  9.2 70.1 %collective-permute-start.2 = (bf16[4,64,4096]{2,1,0:T(8,128)(2,1)}, bf16[4,64,4096]{2,1,0:T(8,128)(2,1)}, u32[]{:S(2)}, u32[]{:S(2)}) collective-permute-start(bf16[4,64,4096]{2,1,0:T(8,128)(2,1)} %param.1), channel_id=1, source_target_pairs={{0,2},{1,3},{2,4},{3,5},{4,6},{5,7},{6,0},{7,1},{8,10},{9,11},{10,... | collective-permute-start | bytes 6291464 | tf_op jit(solution)/shard_map/ppermute | solution.py:17
  127.4 6.0 %copy-start = (f32[64,64,256]{2,1,0:T(8,128)S(1)}, f32[64,64,256]{2,1,0:T(8,128)}, u32[]{:S(2)}) copy-start(f32[64,64,256]{2,1,0:T(8,128)} %tile.14) | copy-start | bytes 12582916
  183.7 98.1 %collective-permute-start.3 = (f32[4,64,4096]{2,1,0:T(8,128)}, f32[4,64,4096]{2,1,0:T(8,128)}, u32[]{:S(2)}, u32[]{:S(2)}) collective-permute-start(f32[4,64,4096]{2,1,0:T(8,128)} %get-tuple-element.6), channel_id=1, source_target_pairs={{0,6},{1,7},{2,0},{3,1},{4,2},{5,3},{6,4},{7,5},{8,14},{9,15},{10,... | collective-permute-start | bytes 12582920 | tf_op jit(solution)/shard_map/ppermute | solution.py:17
  227.4 6.1 %copy-start.1 = (f32[64,64,256]{2,1,0:T(8,128)S(1)}, f32[64,64,256]{2,1,0:T(8,128)}, u32[]{:S(2)}) copy-start(f32[64,64,256]{2,1,0:T(8,128)} %tile.14) | copy-start | bytes 12582916
  281.8 48.0 %collective-permute-start.1 = (f32[4,64,4096]{2,1,0:T(8,128)S(1)}, f32[4,64,4096]{2,1,0:T(8,128)S(1)}, u32[]{:S(2)}, u32[]{:S(2)}) collective-permute-start(f32[4,64,4096]{2,1,0:T(8,128)S(1)} %get-tuple-element.8), channel_id=1, source_target_pairs={{0,7},{1,0},{2,1},{3,2},{4,3},{5,4},{6,5},{7,6},{8,15},{9,8},{10,9... | collective-permute-start | bytes 12582920 | tf_op jit(solution)/shard_map/ppermute | solution.py:17
Sparse Core Ops, SparseCore 0:
  337.1 52.1 reduce-scatter.1
where the time goes:
time: 402 us; the launch traced here: 396 us
  waiting for transfers between devices  152 us (38%)
  local copies, waits for them, and re-layouts  132 us (33%)
  matrix products  66 us (16%)
  other arithmetic  26.8 us (7%)
  between operations  13.9 us (3%)
  starting transfers between devices  6.06 us (2%)
    ppermute x4, waiting for transfers between devices, from_behind(): lax.ppermute(shard, axis, [(i, (i + by) % count) for i in range(count)])  99.3 us
    reduce_scatter x1, waiting for transfers between devices, body(): return lax.psum_scatter(buffer, 'grp', scatter_dimension=1, tiled=True)  52.3 us
    reshape x4, local copies, waits for them, and re-layouts, potentials_of(): density.reshape(visits, grid, grid, grid).transpose(1, 2, 0, 3)  45.3 us
    reshape x4, local copies, waits for them, and re-layouts, potentials_of(): result.reshape(grid, grid, visits, grid).transpose(2, 0, 1, 3)  32.3 us
    dot_general x4, matrix products, hartley_pass(): jnp.einsum('xyc,xk->kyc', values, hartley, precision=lax.Precision.HIGHEST)  26.2 us
    dot_general x4, matrix products, hartley_pass(): jnp.einsum('xyc,cd->xyd', values, block_table, precision=lax.Precision.HI...  23.7 us
    transpose x2, local copies, waits for them, and re-layouts, potentials_of(): result.reshape(grid, grid, visits, grid).transpose(2, 0, 1, 3)  22.9 us
    reshape x2, local copies, waits for them, and re-layouts, potentials_of(): density = density.reshape(visits, grid, grid, grid).transpose(1, 2, 0, 3)...  17.5 us
  transfers between devices with their start and end apart: 5, of which 4 were waited for; matrix products, arithmetic and copies ran while one was open for 29% of the time, Pallas kernels for 0%

commit v1 on v0

v1 whole, which is shorter than its diff:
```python
import functools
import math

import jax
import jax.numpy as jnp
import ml_dtypes
import numpy as np
from jax import lax
from jax.experimental import pallas as pl
from jax.experimental.pallas import tpu as pltpu
from jax.sharding import PartitionSpec as P

ROUNDS = 2


CELL_LENGTH = 41.05
SCREENING = 0.106
LANES = 128


def from_behind(shard, axis, by):
    count = lax.axis_size(axis)
    return lax.ppermute(shard, axis, [(i, (i + by) % count) for i in range(count)])


def kernel_table(grid):
    wavenum = np.arange(grid, dtype=np.float64)
    wavenum = np.where(wavenum < grid // 2, wavenum, wavenum - grid) * (2.0 * math.pi / CELL_LENGTH)
    squared = (
        wavenum[:, None, None] ** 2 + wavenum[None, :, None] ** 2 + wavenum[None, None, :] ** 2
    )
    safe = np.where(squared > 0, squared, 1.0)
    screened = 4.0 * math.pi * (1.0 - np.exp(-safe / (4.0 * SCREENING * SCREENING))) / safe
    return np.where(squared > 0, screened, math.pi / (SCREENING * SCREENING))


def tables(grid, copies):
    indices = np.arange(grid)
    angles = (indices[:, None] * indices[None, :] % grid) * (2.0 * math.pi / grid)
    wide = np.kron(np.eye(copies), np.cos(angles) + np.sin(angles))
    high = wide.astype(ml_dtypes.bfloat16)
    low = (wide - high.astype(np.float64)).astype(ml_dtypes.bfloat16)
    return np.concatenate([high, high, low], axis=1)


def parts_of(values, axis):
    high = values.astype(jnp.bfloat16)
    low = (values - high.astype(jnp.float32)).astype(jnp.bfloat16)
    return jnp.concatenate([high, low, high], axis=axis)


def dot(a, b, dims=((1,), (0,))):
    return lax.dot_general(a, b, (dims, ((), ())), preferred_element_type=jnp.float32)


def pair_kernel(grid, step, own_ref, visit_ref, table_ref, right_ref, wide_ref, slim_ref, *rest):
    if len(rest) == 5:
        before_ref, home_ref, back_ref, t_ref, u_ref = rest
    else:
        before_ref = None
        home_ref, back_ref, t_ref, u_ref = rest
    count, _, plane = own_ref.shape
    width = count * grid
    lines = step // grid
    halves = width // LANES

    def forward(c, _):
        lanes = pl.ds(pl.multiple_of(c * step, step), step)
        visit = visit_ref[:, lanes].astype(jnp.float32)
        density = jnp.concatenate(
            [own_ref[n, :, lanes].astype(jnp.float32) * visit for n in range(count)], axis=0
        )
        turned = dot(parts_of(density.T, 1), right_ref[...], ((1,), (1,)))
        turned = dot(wide_ref[...], parts_of(turned, 0))
        for j in range(lines):
            for h in range(halves):
                t_ref[h, pl.ds(c * lines + j, grid, stride=grid), :] = turned[
                    j * grid : (j + 1) * grid, h * LANES : (h + 1) * LANES
                ]
        return 0

    lax.fori_loop(0, plane // step, forward, 0)

    def middle(k, _):
        for j in range(lines):
            row = k * lines + j
            rows = pl.ds(pl.multiple_of(row * grid, grid), grid)
            values = jnp.concatenate([t_ref[h, rows, :] for h in range(halves)], axis=1)
            scale = jnp.concatenate([table_ref[rows, :]] * halves, axis=1)
            values = dot(slim_ref[...], parts_of(values, 0)) * scale
            values = dot(slim_ref[...], parts_of(values, 0))
            for h in range(halves):
                u_ref[h, pl.ds(row, grid, stride=grid), :] = values[:, h * LANES : (h + 1) * LANES]
        return 0

    lax.fori_loop(0, grid // lines, middle, 0)

    def backward(c, _):
        lanes = pl.ds(pl.multiple_of(c * step, step), step)
        values = jnp.concatenate([u_ref[h, lanes, :] for h in range(halves)], axis=1)
        values = dot(wide_ref[...], parts_of(values, 0))
        potential = dot(right_ref[...], parts_of(values, 1), ((1,), (1,)))
        visit = visit_ref[:, lanes].astype(jnp.float32)
        total = None
        for n in range(count):
            one = potential[n * grid : (n + 1) * grid, :]
            term = visit * one
            if before_ref is not None:
                term = term + before_ref[n, :, lanes]
            home_ref[n, :, lanes] = term
            term = own_ref[n, :, lanes].astype(jnp.float32) * one
            total = term if total is None else total + term
        back_ref[:, lanes] = total
        return 0

    lax.fori_loop(0, plane // step, backward, 0)


def pairs(own, visit, before, consts):
    count, grid, plane = own.shape
    step = 4 * grid
    width = count * grid
    extra = () if before is None else (before,)
    vmem = pl.BlockSpec(memory_space=pltpu.VMEM)
    return pl.pallas_call(
        functools.partial(pair_kernel, grid, step),
        out_shape=(
            jax.ShapeDtypeStruct((count, grid, plane), jnp.float32),
            jax.ShapeDtypeStruct((grid, plane), jnp.float32),
        ),
        in_specs=[vmem] * (6 + len(extra)),
        out_specs=(vmem, vmem),
        scratch_shapes=[
            pltpu.VMEM((width // LANES, grid * grid, LANES), jnp.float32),
            pltpu.VMEM((width // LANES, grid * grid, LANES), jnp.float32),
        ],
        cost_estimate=pl.CostEstimate(
            flops=36 * plane * width * step, bytes_accessed=16 * count * grid * plane, transcendentals=0
        ),
        compiler_params=pltpu.CompilerParams(vmem_limit_bytes=48 * 1024 * 1024),
    )(own, visit, *consts, *extra)


def body(orbitals):
    own_count, grid, plane = orbitals.shape
    groups = lax.axis_size("grp")
    split_count = groups // own_count
    count = own_count // split_count
    group_index = lax.axis_index("grp")
    band_row = group_index // split_count
    own_start = group_index % split_count * count
    own = orbitals if count == own_count else lax.dynamic_slice_in_dim(orbitals, own_start, count, 0)
    outgoing = lax.dynamic_index_in_dim(orbitals, band_row, 0, keepdims=False)
    table = kernel_table(grid).reshape(grid * grid, grid) * (-0.25 / float(grid**3))
    consts = (
        jnp.asarray(np.tile(table, (1, LANES // grid)).astype(np.float32)),
        jnp.asarray(tables(grid, count)),
        jnp.asarray(tables(grid, 4)),
        jnp.asarray(tables(grid, 1)),
    )
    home = None
    returned = None
    arrivals = [from_behind(outgoing, "band", d) for d in range(1, ROUNDS + 1)]
    for distance in range(1, ROUNDS + 1):
        home, back = pairs(own, arrivals[distance - 1], home, consts)
        back = from_behind(back, "band", -distance)
        returned = back if returned is None else returned + back
    zeros = jnp.zeros((own_count, grid, plane), jnp.float32)
    buffer = home if count == own_count else lax.dynamic_update_slice(zeros, home, (own_start, 0, 0))
    mine = jnp.arange(own_count)[:, None, None] == band_row
    buffer = buffer + jnp.where(mine, returned[None], 0.0)
    return lax.psum_scatter(buffer, "grp", scatter_dimension=1, tiled=True)


def solution(mesh):
    return jax.shard_map(
        body,
        mesh=mesh,
        in_specs=(P("band", None, None),),
        out_specs=P("band", "grp", None),
        check_vma=False,
    )
```

time: 402 us -> 204 us (0.51); the launches traced: 396 us -> 203 us
  local copies, waits for them, and re-layouts: 132 us -> 6.07 us
  Pallas kernels: 0 us -> 74.6 us
  matrix products: 66 us -> 0 us
  waiting for transfers between devices: 152 us -> 95.2 us
  other arithmetic: 26.8 us -> 4.85 us
    reshape x10 -> x0, local copies, waits for them, and re-layouts: 95.2 us -> none  [the longest x4 45.3 us: potentials_of(): density.reshape(visits, grid, grid, grid).transpose(1, 2, 0, 3)]
    pallas_call x0 -> x2, Pallas kernels: none -> 74.6 us  [pairs(): pl.pallas_call(functools.partial(pair_kernel, grid, step), out_shape=(jax...]
    dot_general x12 -> x0, matrix products: 66 us -> none  [the longest x4 26.2 us: hartley_pass(): jnp.einsum('xyc,xk->kyc', values, hartley, precision=lax.Precision.HIGHEST)]
    ppermute x4, waiting for transfers between devices: 99.3 us -> 41.1 us  [from_behind(): lax.ppermute(shard, axis, [(i, (i + by) % count) for i in range(count)])]
    transpose x2 -> x0, local copies, waits for them, and re-layouts: 22.9 us -> none  [potentials_of(): result.reshape(grid, grid, visits, grid).transpose(2, 0, 1, 3)]
    another operation x2 -> x0, local copies, waits for them, and re-layouts: 13.5 us -> none  [body(): kernel_wide = jnp.tile(kernel_table(grid), (1, 1, visits))]
    reduce_sum x2 -> x0, other arithmetic: 9.53 us -> none  [body(): jnp.sum(arrived.astype(jnp.float32) * potentials, axis=0)]
    mul x4 -> x0, other arithmetic: 8.99 us -> none  [the longest x2 7.73 us: potentials_of(): density = own_band.astype(jnp.float32)[None] * arrived.astype(jnp.float32)]
  transfers between devices with their start and end apart: 5 -> 5, of which waited for: 4 -> 4; matrix products, arithmetic and copies ran while one was open for 29% -> 0% of each run, Pallas kernels for 0% -> 18%
where the time goes in v1:
time: 204 us; the launch traced here: 203 us
  waiting for transfers between devices  95.2 us (47%)
  Pallas kernels  74.6 us (37%)
  between operations  13.4 us (7%)
  starting transfers between devices  8.94 us (4%)
  local copies, waits for them, and re-layouts  6.07 us (3%)
  other arithmetic  4.85 us (2%)
    pallas_call x2, Pallas kernels, pairs(): pl.pallas_call(functools.partial(pair_kernel, grid, step), out_shape=(jax...  74.6 us
    reduce_scatter x1, waiting for transfers between devices, body(): return lax.psum_scatter(buffer, 'grp', scatter_dimension=1, tiled=True)  54.1 us
    ppermute x4, waiting for transfers between devices, from_behind(): lax.ppermute(shard, axis, [(i, (i + by) % count) for i in range(count)])  41.1 us
    ppermute x4, starting transfers between devices, from_behind(): lax.ppermute(shard, axis, [(i, (i + by) % count) for i in range(count)])  8.94 us
    unnamed x12, local copies, waits for them, and re-layouts  4.94 us
    add x1, other arithmetic, body(): buffer = buffer + jnp.where(mine, returned[None], 0.0)  4.74 us
  transfers between devices with their start and end apart: 5, of which 4 were waited for; matrix products, arithmetic and copies ran while one was open for 0% of the time, Pallas kernels for 18%

profile of v1, /device:TPU:1, one launch (start us, length us, event | category | flops | bytes accessed | tf_op | source)
XLA Modules:
  0.0 203.0 jit_solution(17673481895952349875)
XLA Ops:
  6.5 0.0 reduce-scatter.2.cloned.1.call-start
  6.5 0.0 copy-start.3
  6.5 0.0 copy-start.5
  6.5 1.1 dynamic-slice_bitcast_fusion
  7.7 2.7 %collective-permute-start.1 = (bf16[64,4096]{1,0:T(8,128)(2,1)S(1)}, bf16[64,4096]{1,0:T(8,128)(2,1)S(1)}, u32[]{:S(2)}, u32[]{:S(2)}) collective-permute-start(bf16[64,4096]{1,0:T(8,128)(2,1)S(1)} %dynamic-slice_bitcast_fusion), channel_id=1, source_target_pairs={{0,1},{1,2},{2,3},{3,4},{4,5},{5,6},{6,7},{7,0},{8,9},{9,10},{10,1... | collective-permute-start | bytes 1572872 | tf_op jit(solution)/shard_map/ppermute | solution.py:23
  10.4 1.3 collective-permute-start
  11.7 9.9 %collective-permute-done.1.visit_ref = bf16[64,4096]{1,0:T(8,128)(2,1)S(1)} collective-permute-done((bf16[64,4096]{1,0:T(8,128)(2,1)S(1)}, bf16[64,4096]{1,0:T(8,128)(2,1)S(1)}, u32[]{:S(2)}, u32[]{:S(2)}) %collective-permute-start.1) | collective-permute-done | bytes 524320 | tf_op jit(solution)/shard_map/ppermute | solution.py:23
  21.6 0.0 copy-start
  21.6 1.6 copy-done
  23.2 0.0 copy-start.1
  23.2 1.6 copy-done.1
  24.7 0.0 copy-start.2
  24.8 1.0 copy-done.2
  25.7 0.0 copy-start.4
  25.7 0.8 copy-done.4
  26.5 36.2 %shard_map.55 = (f32[4,64,4096]{2,1,0:T(8,128)}, f32[64,4096]{1,0:T(8,128)S(1)}) custom-call(bf16[4,64,4096]{2,1,0:T(8,128)(2,1)S(1)} %copy-done, bf16[64,4096]{1,0:T(8,128)(2,1)S(1)} %collective-permute-done.1.visit_ref, f32[4096,128]{1,0:T(8,128)S(1)} %copy-done.1, bf16[256,768]{1,0:T(8,128)(2,1)S(1)} %copy-done.2, bf16[256,768]{1,0:T(8,128)(2,1)S(1)} %copy-done.2, ...), custom_call_target="tpu_custom_call" | custom-call | flops 9663676416 | bytes 16777216 | tf_op jit(solution)/shard_map/pallas_call | solution.py:125
  62.7 0.0 collective-permute-done.visit_ref
  62.7 0.0 copy-done.3
  62.7 0.0 copy-done.5
  62.7 38.4 %shard_map.56 = (f32[4,64,4096]{2,1,0:T(8,128)}, f32[64,4096]{1,0:T(8,128)S(1)}) custom-call(bf16[4,64,4096]{2,1,0:T(8,128)(2,1)S(1)} %copy-done, bf16[64,4096]{1,0:T(8,128)(2,1)S(1)} %collective-permute-done.visit_ref, f32[4096,128]{1,0:T(8,128)S(1)} %copy-done.1, bf16[256,768]{1,0:T(8,128)(2,1)S(1)} %copy-done.3, bf16[256,768]{1,0:T(8,128)(2,1)S(1)} %copy-done.3, ...), custom_call_target="tpu_custom_call" | custom-call | flops 9663676416 | bytes 16777216 | tf_op jit(solution)/shard_map/pallas_call | solution.py:125
  101.1 1.2 collective-permute-start.3
  102.3 3.7 %collective-permute-start.2 = (f32[64,4096]{1,0:T(8,128)S(1)}, f32[64,4096]{1,0:T(8,128)S(1)}, u32[]{:S(2)}, u32[]{:S(2)}) collective-permute-start(f32[64,4096]{1,0:T(8,128)S(1)} %get-tuple-element.11), channel_id=1, source_target_pairs={{0,7},{1,0},{2,1},{3,2},{4,3},{5,4},{6,5},{7,6},{8,15},{9,8},{10,9... | collective-permute-start | bytes 3145736 | tf_op jit(solution)/shard_map/ppermute | solution.py:23
  106.0 17.5 %collective-permute-done.3 = f32[64,4096]{1,0:T(8,128)S(1)} collective-permute-done((f32[64,4096]{1,0:T(8,128)S(1)}, f32[64,4096]{1,0:T(8,128)S(1)}, u32[]{:S(2)}, u32[]{:S(2)}) %collective-permute-start.3) | collective-permute-done | bytes 1048608 | tf_op jit(solution)/shard_map/ppermute | solution.py:23
  123.5 13.7 %collective-permute-done.2 = f32[64,4096]{1,0:T(8,128)S(1)} collective-permute-done((f32[64,4096]{1,0:T(8,128)S(1)}, f32[64,4096]{1,0:T(8,128)S(1)}, u32[]{:S(2)}, u32[]{:S(2)}) %collective-permute-start.2) | collective-permute-done | bytes 1048608 | tf_op jit(solution)/shard_map/ppermute | solution.py:23
  137.2 0.1 add.14
  137.3 4.7 %select_add_fusion = f32[4,64,4096]{2,1,0:T(8,128)} fusion(f32[4,64,4096]{2,1,0:T(8,128)} %get-tuple-element.10, f32[64,4096]{1,0:T(8,128)S(1)} %add.14, pred[4]{0:T(512)(128)(4,1)S(1)} %iota_compare_fusion), kind=kLoop, calls=%fused_computation | loop fusion | flops 2097152 | bytes 9437188 | tf_op jit(solution)/shard_map/add | solution.py:171
  142.1 0.0 reduce-scatter.2.cloned.1.call-update
  142.1 54.1 %reduce-scatter.2.cloned.1.call-done = f32[4,16,4096]{2,1,0:T(8,128)} async-done(((f32[4,64,4096]{2,1,0:T(8,128)}), f32[4,16,4096]{2,1,0:T(8,128)}) %reduce-scatter.2.cloned.1.call-update) | async-done | bytes 1048592 | tf_op jit(solution)/shard_map/reduce_scatter | solution.py:172
  (1 shorter events, 0.0 us)
Async XLA Ops:
  6.5 189.6 %reduce-scatter.2.cloned.1.call-start = ((), (), s32[]{:S(2)}) async-start(), calls=%async_computation.1 | async-start | bytes 5242880 | tf_op jit(solution)/shard_map/reduce_scatter | solution.py:172
  6.5 56.2 %copy-start.3 = (bf16[256,768]{1,0:T(8,128)(2,1)S(1)}, bf16[256,768]{1,0:T(8,128)(2,1)}, u32[]{:S(2)}) copy-start(bf16[256,768]{1,0:T(8,128)(2,1)} %constant.31.clone.right_ref.wide_ref) | copy-start | bytes 1179652
  6.5 56.2 %copy-start.5 = (bf16[64,192]{1,0:T(8,128)(2,1)S(1)}, bf16[64,192]{1,0:T(8,128)(2,1)}, u32[]{:S(2)}) copy-start(bf16[64,192]{1,0:T(8,128)(2,1)} %constant.32.clone.slim_ref) | copy-start | bytes 73732
  7.7 13.9 %collective-permute-start.1 = (bf16[64,4096]{1,0:T(8,128)(2,1)S(1)}, bf16[64,4096]{1,0:T(8,128)(2,1)S(1)}, u32[]{:S(2)}, u32[]{:S(2)}) collective-permute-start(bf16[64,4096]{1,0:T(8,128)(2,1)S(1)} %dynamic-slice_bitcast_fusion), channel_id=1, source_target_pairs={{0,1},{1,2},{2,3},{3,4},{4,5},{5,6},{6,7},{7,0},{8,9},{9,10},{10,1... | collective-permute-start | bytes 1572872 | tf_op jit(solution)/shard_map/ppermute | solution.py:23
  10.4 52.3 %collective-permute-start = (bf16[64,4096]{1,0:T(8,128)(2,1)S(1)}, bf16[64,4096]{1,0:T(8,128)(2,1)S(1)}, u32[]{:S(2)}, u32[]{:S(2)}) collective-permute-start(bf16[64,4096]{1,0:T(8,128)(2,1)S(1)} %dynamic-slice_bitcast_fusion), channel_id=1, source_target_pairs={{0,2},{1,3},{2,4},{3,5},{4,6},{5,7},{6,0},{7,1},{8,10},{9,11},{10,... | collective-permute-start | bytes 1572872 | tf_op jit(solution)/shard_map/ppermute | solution.py:23
  21.6 1.6 copy-start
  23.2 1.6 copy-start.1
  24.7 1.0 copy-start.2
  25.7 0.8 copy-start.4
  101.1 22.4 %collective-permute-start.3 = (f32[64,4096]{1,0:T(8,128)S(1)}, f32[64,4096]{1,0:T(8,128)S(1)}, u32[]{:S(2)}, u32[]{:S(2)}) collective-permute-start(f32[64,4096]{1,0:T(8,128)S(1)} %get-tuple-element.12), channel_id=1, source_target_pairs={{0,6},{1,7},{2,0},{3,1},{4,2},{5,3},{6,4},{7,5},{8,14},{9,15},{10,... | collective-permute-start | bytes 3145736 | tf_op jit(solution)/shard_map/ppermute | solution.py:23
  102.3 35.0 %collective-permute-start.2 = (f32[64,4096]{1,0:T(8,128)S(1)}, f32[64,4096]{1,0:T(8,128)S(1)}, u32[]{:S(2)}, u32[]{:S(2)}) collective-permute-start(f32[64,4096]{1,0:T(8,128)S(1)} %get-tuple-element.11), channel_id=1, source_target_pairs={{0,7},{1,0},{2,1},{3,2},{4,3},{5,4},{6,5},{7,6},{8,15},{9,8},{10,9... | collective-permute-start | bytes 3145736 | tf_op jit(solution)/shard_map/ppermute | solution.py:23
Sparse Core Ops, SparseCore 0:
  142.2 53.9 reduce-scatter.1

commit v2 on v1

v2 whole, which is shorter than its diff:
```python
import functools
import math

import jax
import jax.numpy as jnp
import ml_dtypes
import numpy as np
from jax import lax
from jax.experimental import pallas as pl
from jax.experimental.pallas import tpu as pltpu
from jax.sharding import PartitionSpec as P

ROUNDS = 2


CELL_LENGTH = 41.05
SCREENING = 0.106
LANES = 128
PARTS = 2
MESH = pl.DeviceIdType.MESH


def kernel_table(grid):
    wavenum = np.arange(grid, dtype=np.float64)
    wavenum = np.where(wavenum < grid // 2, wavenum, wavenum - grid) * (2.0 * math.pi / CELL_LENGTH)
    squared = (
        wavenum[:, None, None] ** 2 + wavenum[None, :, None] ** 2 + wavenum[None, None, :] ** 2
    )
    safe = np.where(squared > 0, squared, 1.0)
    screened = 4.0 * math.pi * (1.0 - np.exp(-safe / (4.0 * SCREENING * SCREENING))) / safe
    return np.where(squared > 0, screened, math.pi / (SCREENING * SCREENING))


def tables(grid, copies):
    indices = np.arange(grid)
    angles = (indices[:, None] * indices[None, :] % grid) * (2.0 * math.pi / grid)
    wide = np.kron(np.eye(copies), np.cos(angles) + np.sin(angles))
    high = wide.astype(ml_dtypes.bfloat16)
    low = (wide - high.astype(np.float64)).astype(ml_dtypes.bfloat16)
    return np.concatenate([high, high, low], axis=1)


def parts_of(values, axis):
    high = values.astype(jnp.bfloat16)
    low = (values - high.astype(jnp.float32)).astype(jnp.bfloat16)
    return jnp.concatenate([high, low, high], axis=axis)


def dot(a, b, dims=((1,), (0,))):
    return lax.dot_general(a, b, (dims, ((), ())), preferred_element_type=jnp.float32)


def exchange_kernel(
    grid,
    step,
    groups,
    ring,
    orbitals_ref,
    table_ref,
    right_ref,
    wide_ref,
    slim_ref,
    out_ref,
    visit_ref,
    home_ref,
    back_ref,
    home_got,
    back_got,
    t_ref,
    u_ref,
    in_send,
    in_recv,
    home_send,
    home_recv,
    back_send,
    back_recv,
):
    own_count, _, plane = orbitals_ref.shape
    split_count = groups // own_count
    count = own_count // split_count
    planes = grid // groups
    width = count * grid
    lines = step // grid
    halves = width // LANES
    part = plane // PARTS
    group, band = lax.axis_index("grp"), lax.axis_index("band")
    band_row = group // split_count
    own_start = lax.rem(group, split_count) * count

    def device(by, along):
        return (lax.rem(group + by, groups), lax.rem(band + along + ring, ring))

    barrier = pltpu.get_barrier_semaphore()
    greeted = 0
    for along in range(-ROUNDS, ROUNDS + 1):
        for by in range(groups):
            if by or along:
                pl.semaphore_signal(
                    barrier, inc=1, device_id=device(by, along), device_id_type=MESH
                )
                greeted += 1
    pl.semaphore_wait(barrier, greeted)

    def remote(source, target, send, recv, where):
        copy = pltpu.make_async_remote_copy(
            src_ref=source,
            dst_ref=target,
            send_sem=send,
            recv_sem=recv,
            device_id=where,
            device_id_type=MESH,
        )
        copy.start()
        return copy

    def lanes_of(p):
        return pl.ds(p * part, part)

    def rows_of(by):
        return pl.ds(pl.multiple_of(lax.rem(group + by, groups) * planes, planes), planes)

    arrivals = [
        [
            remote(
                orbitals_ref.at[band_row, :, lanes_of(p)],
                visit_ref.at[d, :, lanes_of(p)],
                in_send.at[d, p],
                in_recv.at[d, p],
                device(0, d + 1),
            )
            for p in range(PARTS)
        ]
        for d in range(ROUNDS)
    ]

    def own_of(n, lanes):
        return orbitals_ref[own_start + n, :, lanes].astype(jnp.float32)

    def forward(d, c, _):
        lanes = pl.ds(pl.multiple_of(c * step, step), step)
        visit = visit_ref[d, :, lanes].astype(jnp.float32)
        density = jnp.concatenate([own_of(n, lanes) * visit for n in range(count)], axis=0)
        turned = dot(parts_of(density.T, 1), right_ref[...], ((1,), (1,)))
        turned = dot(wide_ref[...], parts_of(turned, 0))
        for j in range(lines):
            for h in range(halves):
                t_ref[h, pl.ds(c * lines + j, grid, stride=grid), :] = turned[
                    j * grid : (j + 1) * grid, h * LANES : (h + 1) * LANES
                ]
        return 0

    def middle(k, _):
        for j in range(lines):
            row = k * lines + j
            rows = pl.ds(pl.multiple_of(row * grid, grid), grid)
            values = jnp.concatenate([t_ref[h, rows, :] for h in range(halves)], axis=1)
            scale = jnp.concatenate([table_ref[rows, :]] * halves, axis=1)
            values = dot(slim_ref[...], parts_of(values, 0)) * scale
            values = dot(slim_ref[...], parts_of(values, 0))
            for h in range(halves):
                u_ref[h, pl.ds(row, grid, stride=grid), :] = values[:, h * LANES : (h + 1) * LANES]
        return 0

    def backward(d, c, _):
        lanes = pl.ds(pl.multiple_of(c * step, step), step)
        values = jnp.concatenate([u_ref[h, lanes, :] for h in range(halves)], axis=1)
        values = dot(wide_ref[...], parts_of(values, 0))
        potential = dot(right_ref[...], parts_of(values, 1), ((1,), (1,)))
        visit = visit_ref[d, :, lanes].astype(jnp.float32)
        total = None
        for n in range(count):
            one = potential[n * grid : (n + 1) * grid, :]
            term = visit * one
            if d > 0:
                term = term + home_ref[n, :, lanes]
            home_ref[n, :, lanes] = term
            term = own_of(n, lanes) * one
            total = term if total is None else total + term
        back_ref[d, :, lanes] = total
        return 0

    chunks = part // step
    home_copies = [[] for _ in range(PARTS)]
    back_copies = [[[] for _ in range(PARTS)] for _ in range(ROUNDS)]
    for d in range(ROUNDS):
        for p in range(PARTS):
            arrivals[d][p].wait_recv()
            lax.fori_loop(p * chunks, (p + 1) * chunks, functools.partial(forward, d), 0)
        lax.fori_loop(0, grid // lines, middle, 0)
        for p in range(PARTS):
            lax.fori_loop(p * chunks, (p + 1) * chunks, functools.partial(backward, d), 0)
            lanes = lanes_of(p)
            for by in range(groups):
                back_copies[d][p].append(
                    remote(
                        back_ref.at[d, rows_of(by), lanes],
                        back_got.at[d, by, :, lanes],
                        back_send.at[d, by, p],
                        back_recv.at[d, by, p],
                        device(by, -d - 1),
                    )
                )
            if d == ROUNDS - 1:
                for by in range(1, groups):
                    home_copies[p].append(
                        remote(
                            home_ref.at[:, rows_of(by), lanes],
                            home_got.at[by - 1, :, :, lanes],
                            home_send.at[by - 1, p],
                            home_recv.at[by - 1, p],
                            device(by, 0),
                        )
                    )

    if count < own_count:
        out_ref[...] = jnp.zeros_like(out_ref)
    out_ref[pl.ds(own_start, count)] = home_ref[:, rows_of(0), :]
    for d in range(ROUNDS):
        for p in range(PARTS):
            lanes = lanes_of(p)
            if d == ROUNDS - 1:
                for by in range(1, groups):
                    home_copies[p][by - 1].wait_recv()
                    source = lax.rem(group + groups - by, groups)
                    start = lax.rem(source, split_count) * count
                    out_ref[pl.ds(start, count), :, lanes] += home_got[by - 1, :, :, lanes]
            for by in range(groups):
                back_copies[d][p][by].wait_recv()
                row = lax.rem(group + groups - by, groups) // split_count
                out_ref[row, :, lanes] += back_got[d, by, :, lanes]
    for p in range(PARTS):
        for copy in home_copies[p]:
            copy.wait_send()
        for d in range(ROUNDS):
            arrivals[d][p].wait_send()
            for copy in back_copies[d][p]:
                copy.wait_send()


def body(orbitals):
    own_count, grid, plane = orbitals.shape
    groups, ring = lax.axis_size("grp"), lax.axis_size("band")
    count = own_count // (groups // own_count)
    planes = grid // groups
    width = count * grid
    step = 4 * grid
    table = kernel_table(grid).reshape(grid * grid, grid) * (-0.25 / float(grid**3))
    consts = (
        jnp.asarray(np.tile(table, (1, LANES // grid)).astype(np.float32)),
        jnp.asarray(tables(grid, count)),
        jnp.asarray(tables(grid, 4)),
        jnp.asarray(tables(grid, 1)),
    )
    vmem = pl.BlockSpec(memory_space=pltpu.VMEM)
    dma = pltpu.SemaphoreType.DMA
    return pl.pallas_call(
        functools.partial(exchange_kernel, grid, step, groups, ring),
        out_shape=jax.ShapeDtypeStruct((own_count, planes, plane), jnp.float32),
        in_specs=[vmem] * 5,
        out_specs=vmem,
        scratch_shapes=[
            pltpu.VMEM((ROUNDS, grid, plane), jnp.bfloat16),
            pltpu.VMEM((count, grid, plane), jnp.float32),
            pltpu.VMEM((ROUNDS, grid, plane), jnp.float32),
            pltpu.VMEM((groups - 1, count, planes, plane), jnp.float32),
            pltpu.VMEM((ROUNDS, groups, planes, plane), jnp.float32),
            pltpu.VMEM((width // LANES, grid * grid, LANES), jnp.float32),
            pltpu.VMEM((width // LANES, grid * grid, LANES), jnp.float32),
            dma((ROUNDS, PARTS)),
            dma((ROUNDS, PARTS)),
            dma((groups - 1, PARTS)),
            dma((groups - 1, PARTS)),
            dma((ROUNDS, groups, PARTS)),
            dma((ROUNDS, groups, PARTS)),
        ],
        compiler_params=pltpu.CompilerParams(
            collective_id=0, has_side_effects=True, vmem_limit_bytes=48 * 1024 * 1024
        ),
    )(orbitals, *consts)


def solution(mesh):
    return jax.shard_map(
        body,
        mesh=mesh,
        in_specs=(P("band", None, None),),
        out_specs=P("band", "grp", None),
        check_vma=False,
    )
```

time: 204 us -> 137 us (0.67)
  waiting for transfers between devices: 95.2 us -> 0 us
  Pallas kernels: 74.6 us -> 129 us
  between operations: 13.4 us -> 0.01 us
  starting transfers between devices: 8.94 us -> 0 us
  other arithmetic: 4.85 us -> 0 us
    pallas_call x2 -> x1, Pallas kernels: 74.6 us -> 129 us  [body(): pl.pallas_call(functools.partial(exchange_kernel, grid, step, groups, rin...]
    reduce_scatter x1 -> x0, waiting for transfers between devices: 54.1 us -> none  [body(): return lax.psum_scatter(buffer, 'grp', scatter_dimension=1, tiled=True)]
    ppermute x4 -> x0, waiting for transfers between devices: 41.1 us -> none  [from_behind(): lax.ppermute(shard, axis, [(i, (i + by) % count) for i in range(count)])]
    ppermute x4 -> x0, starting transfers between devices: 8.94 us -> none  [from_behind(): lax.ppermute(shard, axis, [(i, (i + by) % count) for i in range(count)])]
    add x2 -> x0, other arithmetic: 4.85 us -> none  [the longest x1 4.74 us: body(): buffer = buffer + jnp.where(mine, returned[None], 0.0)]
    unnamed x12 -> x9, local copies, waits for them, and re-layouts: 4.94 us -> 5.91 us
  transfers between devices with their start and end apart: 5 -> 0, of which waited for: 4 -> 0; matrix products, arithmetic and copies ran while one was open for 0% -> 0% of each run, Pallas kernels for 18% -> 0%
where the time goes in v2:
time: 137 us; the launch traced here: 135 us
  Pallas kernels  129 us (94%)
  local copies, waits for them, and re-layouts  5.91 us (4%)
    pallas_call x1, Pallas kernels, body(): pl.pallas_call(functools.partial(exchange_kernel, grid, step, groups, rin...  129 us
    unnamed x9, local copies, waits for them, and re-layouts  5.91 us

profile of v2, /device:TPU:1, one launch (start us, length us, event | category | flops | bytes accessed | tf_op | source)
XLA Modules:
  0.0 135.2 jit_solution(236193044471567828)
XLA Ops:
  0.0 0.0 copy-start
  0.0 1.6 %copy-done = bf16[4,64,4096]{2,1,0:T(8,128)(2,1)S(1)} copy-done((bf16[4,64,4096]{2,1,0:T(8,128)(2,1)S(1)}, bf16[4,64,4096]{2,1,0:T(8,128)(2,1)}, u32[]{:S(2)}) %copy-start) | copy-done | bytes 2097176
  1.6 0.0 copy-start.1
  1.6 1.6 %copy-done.1 = f32[4096,128]{1,0:T(8,128)S(1)} copy-done((f32[4096,128]{1,0:T(8,128)S(1)}, f32[4096,128]{1,0:T(8,128)}, u32[]{:S(2)}) %copy-start.1) | copy-done | bytes 2097176
  3.2 0.0 copy-start.2
  3.2 1.0 copy-done.2
  4.2 0.0 copy-start.3
  4.2 0.8 copy-done.3
  4.9 129.3 %shard_map.55 = f32[4,16,4096]{2,1,0:T(8,128)S(1)} custom-call(bf16[4,64,4096]{2,1,0:T(8,128)(2,1)S(1)} %copy-done, f32[4096,128]{1,0:T(8,128)S(1)} %copy-done.1, bf16[256,768]{1,0:T(8,128)(2,1)S(1)} %copy-done.2, bf16[256,768]{1,0:T(8,128)(2,1)S(1)} %copy-done.2, bf16[64,192]{1,0:T(8,128)(2,1)S(1)} %copy-done.3), custom_call_target="tpu_custom_call" | custom-call | tf_op jit(solution)/shard_map/pallas_call | solution.py:256
  134.2 1.0 copy.7
Async XLA Ops:
  0.0 1.6 %copy-start = (bf16[4,64,4096]{2,1,0:T(8,128)(2,1)S(1)}, bf16[4,64,4096]{2,1,0:T(8,128)(2,1)}, u32[]{:S(2)}) copy-start(bf16[4,64,4096]{2,1,0:T(8,128)(2,1)} %orbitals_ref.1) | copy-start | bytes 6291460
  1.6 1.6 %copy-start.1 = (f32[4096,128]{1,0:T(8,128)S(1)}, f32[4096,128]{1,0:T(8,128)}, u32[]{:S(2)}) copy-start(f32[4096,128]{1,0:T(8,128)} %constant.6.clone.table_ref) | copy-start | bytes 6291460
  3.2 1.0 copy-start.2
  4.2 0.8 copy-start.3

commit v3 on v2

--- a/solution.py
+++ b/solution.py
@@ -16,7 +16,8 @@
 CELL_LENGTH = 41.05
 SCREENING = 0.106
 LANES = 128
-PARTS = 2
+PARTS = 4
+UNROLL = 4
 MESH = pl.DeviceIdType.MESH
 
 
@@ -56,11 +57,14 @@
     groups,
     ring,
     orbitals_ref,
+    table_hbm,
+    right_hbm,
+    slim_hbm,
+    out_ref,
+    own_ref,
     table_ref,
     right_ref,
-    wide_ref,
     slim_ref,
-    out_ref,
     visit_ref,
     home_ref,
     back_ref,
@@ -68,6 +72,7 @@
     back_got,
     t_ref,
     u_ref,
+    local_sem,
     in_send,
     in_recv,
     home_send,
@@ -90,6 +95,15 @@
     def device(by, along):
         return (lax.rem(group + by, groups), lax.rem(band + along + ring, ring))
 
+    locals_ = [
+        pltpu.make_async_copy(orbitals_ref.at[pl.ds(own_start, count)], own_ref, local_sem.at[0]),
+        pltpu.make_async_copy(right_hbm, right_ref, local_sem.at[1]),
+        pltpu.make_async_copy(slim_hbm, slim_ref, local_sem.at[2]),
+        pltpu.make_async_copy(table_hbm, table_ref, local_sem.at[3]),
+    ]
+    for copy in locals_:
+        copy.start()
+
     barrier = pltpu.get_barrier_semaphore()
     greeted = 0
     for along in range(-ROUNDS, ROUNDS + 1):
@@ -134,14 +148,23 @@
     ]
 
     def own_of(n, lanes):
-        return orbitals_ref[own_start + n, :, lanes].astype(jnp.float32)
+        return own_ref[n, :, lanes].astype(jnp.float32)
+
+    def slim_lines(values):
+        return jnp.concatenate(
+            [
+                dot(slim_ref[...], parts_of(values[j * grid : (j + 1) * grid], 0))
+                for j in range(lines)
+            ],
+            axis=0,
+        )
 
     def forward(d, c, _):
         lanes = pl.ds(pl.multiple_of(c * step, step), step)
         visit = visit_ref[d, :, lanes].astype(jnp.float32)
         density = jnp.concatenate([own_of(n, lanes) * visit for n in range(count)], axis=0)
         turned = dot(parts_of(density.T, 1), right_ref[...], ((1,), (1,)))
-        turned = dot(wide_ref[...], parts_of(turned, 0))
+        turned = slim_lines(turned)
         for j in range(lines):
             for h in range(halves):
                 t_ref[h, pl.ds(c * lines + j, grid, stride=grid), :] = turned[
@@ -164,7 +187,7 @@
     def backward(d, c, _):
         lanes = pl.ds(pl.multiple_of(c * step, step), step)
         values = jnp.concatenate([u_ref[h, lanes, :] for h in range(halves)], axis=1)
-        values = dot(wide_ref[...], parts_of(values, 0))
+        values = slim_lines(values)
         potential = dot(right_ref[...], parts_of(values, 1), ((1,), (1,)))
         visit = visit_ref[d, :, lanes].astype(jnp.float32)
         total = None
@@ -182,13 +205,15 @@
     chunks = part // step
     home_copies = [[] for _ in range(PARTS)]
     back_copies = [[[] for _ in range(PARTS)] for _ in range(ROUNDS)]
+    for copy in locals_:
+        copy.wait()
     for d in range(ROUNDS):
         for p in range(PARTS):
             arrivals[d][p].wait_recv()
-            lax.fori_loop(p * chunks, (p + 1) * chunks, functools.partial(forward, d), 0)
-        lax.fori_loop(0, grid // lines, middle, 0)
+            lax.fori_loop(p * chunks, (p + 1) * chunks, functools.partial(forward, d), 0, unroll=UNROLL)
+        lax.fori_loop(0, grid // lines, middle, 0, unroll=UNROLL)
         for p in range(PARTS):
-            lax.fori_loop(p * chunks, (p + 1) * chunks, functools.partial(backward, d), 0)
+            lax.fori_loop(p * chunks, (p + 1) * chunks, functools.partial(backward, d), 0, unroll=UNROLL)
             lanes = lanes_of(p)
             for by in range(groups):
                 back_copies[d][p].append(
@@ -248,7 +273,6 @@
     consts = (
         jnp.asarray(np.tile(table, (1, LANES // grid)).astype(np.float32)),
         jnp.asarray(tables(grid, count)),
-        jnp.asarray(tables(grid, 4)),
         jnp.asarray(tables(grid, 1)),
     )
     vmem = pl.BlockSpec(memory_space=pltpu.VMEM)
@@ -256,9 +280,11 @@
     return pl.pallas_call(
         functools.partial(exchange_kernel, grid, step, groups, ring),
         out_shape=jax.ShapeDtypeStruct((own_count, planes, plane), jnp.float32),
-        in_specs=[vmem] * 5,
+        in_specs=[pl.BlockSpec(memory_space=pl.ANY)] * 4,
         out_specs=vmem,
         scratch_shapes=[
+            pltpu.VMEM((count, grid, plane), jnp.bfloat16),
+            *[pltpu.VMEM(c.shape, c.dtype) for c in consts],
             pltpu.VMEM((ROUNDS, grid, plane), jnp.bfloat16),
             pltpu.VMEM((count, grid, plane), jnp.float32),
             pltpu.VMEM((ROUNDS, grid, plane), jnp.float32),
@@ -266,6 +292,7 @@
             pltpu.VMEM((ROUNDS, groups, planes, plane), jnp.float32),
             pltpu.VMEM((width // LANES, grid * grid, LANES), jnp.float32),
             pltpu.VMEM((width // LANES, grid * grid, LANES), jnp.float32),
+            dma((4,)),
             dma((ROUNDS, PARTS)),
             dma((ROUNDS, PARTS)),
             dma((groups - 1, PARTS)),

time: 137 us -> 108 us (0.79)
  Pallas kernels: 129 us -> 102 us
    pallas_call x1, Pallas kernels: 129 us -> 102 us  [body(): pl.pallas_call(functools.partial(exchange_kernel, grid, step, groups, rin...]
where the time goes in v3:
time: 108 us; the launch traced here: 107 us
  Pallas kernels  102 us (94%)
  local copies, waits for them, and re-layouts  5.91 us (5%)
    pallas_call x1, Pallas kernels, body(): pl.pallas_call(functools.partial(exchange_kernel, grid, step, groups, rin...  102 us
    unnamed x9, local copies, waits for them, and re-layouts  5.91 us

profile of v3, /device:TPU:1, one launch (start us, length us, event | category | flops | bytes accessed | tf_op | source)
XLA Modules:
  0.0 107.5 jit_solution(498002661863376644)
XLA Ops:
  0.0 0.0 copy-start
  0.0 1.6 %copy-done = bf16[4,64,4096]{2,1,0:T(8,128)(2,1)S(1)} copy-done((bf16[4,64,4096]{2,1,0:T(8,128)(2,1)S(1)}, bf16[4,64,4096]{2,1,0:T(8,128)(2,1)}, u32[]{:S(2)}) %copy-start) | copy-done | bytes 2097176
  1.6 0.0 copy-start.1
  1.6 1.6 %copy-done.1 = f32[4096,128]{1,0:T(8,128)S(1)} copy-done((f32[4096,128]{1,0:T(8,128)S(1)}, f32[4096,128]{1,0:T(8,128)}, u32[]{:S(2)}) %copy-start.1) | copy-done | bytes 2097176
  3.2 0.0 copy-start.2
  3.2 1.0 copy-done.2
  4.2 0.0 copy-start.3
  4.2 0.8 copy-done.3
  4.9 101.6 %shard_map.46 = f32[4,16,4096]{2,1,0:T(8,128)S(1)} custom-call(bf16[4,64,4096]{2,1,0:T(8,128)(2,1)S(1)} %copy-done, f32[4096,128]{1,0:T(8,128)S(1)} %copy-done.1, bf16[256,768]{1,0:T(8,128)(2,1)S(1)} %copy-done.2, bf16[64,192]{1,0:T(8,128)(2,1)S(1)} %copy-done.3), custom_call_target="tpu_custom_call" | custom-call | tf_op jit(solution)/shard_map/pallas_call | solution.py:280
  106.5 1.0 copy.6
Async XLA Ops:
  0.0 1.6 %copy-start = (bf16[4,64,4096]{2,1,0:T(8,128)(2,1)S(1)}, bf16[4,64,4096]{2,1,0:T(8,128)(2,1)}, u32[]{:S(2)}) copy-start(bf16[4,64,4096]{2,1,0:T(8,128)(2,1)} %orbitals_ref.1) | copy-start | bytes 6291460
  1.6 1.6 %copy-start.1 = (f32[4096,128]{1,0:T(8,128)S(1)}, f32[4096,128]{1,0:T(8,128)}, u32[]{:S(2)}) copy-start(f32[4096,128]{1,0:T(8,128)} %constant.6.clone.table_hbm) | copy-start | bytes 6291460
  3.2 1.0 copy-start.2
  4.2 0.8 copy-start.3

commit v4 on v3

--- a/solution.py
+++ b/solution.py
@@ -18,6 +18,7 @@
 LANES = 128
 PARTS = 4
 UNROLL = 4
+PAIRS = 4
 MESH = pl.DeviceIdType.MESH
 
 
@@ -49,6 +50,10 @@
 
 def dot(a, b, dims=((1,), (0,))):
     return lax.dot_general(a, b, (dims, ((), ())), preferred_element_type=jnp.float32)
+
+
+def bands_per_set(count):
+    return min(count, PAIRS // ROUNDS)
 
 
 def exchange_kernel(
@@ -84,7 +89,8 @@
     split_count = groups // own_count
     count = own_count // split_count
     planes = grid // groups
-    width = count * grid
+    per_set = bands_per_set(count)
+    width = per_set * ROUNDS * grid
     lines = step // grid
     halves = width // LANES
     part = plane // PARTS
@@ -142,9 +148,9 @@
                 in_recv.at[d, p],
                 device(0, d + 1),
             )
-            for p in range(PARTS)
+            for d in range(ROUNDS)
         ]
-        for d in range(ROUNDS)
+        for p in range(PARTS)
     ]
 
     def own_of(n, lanes):
@@ -159,10 +165,12 @@
             axis=0,
         )
 
-    def forward(d, c, _):
+    def forward(s, c, _):
         lanes = pl.ds(pl.multiple_of(c * step, step), step)
-        visit = visit_ref[d, :, lanes].astype(jnp.float32)
-        density = jnp.concatenate([own_of(n, lanes) * visit for n in range(count)], axis=0)
+        visits = [visit_ref[d, :, lanes].astype(jnp.float32) for d in range(ROUNDS)]
+        density = jnp.concatenate(
+            [own_of(s * per_set + n, lanes) * v for n in range(per_set) for v in visits], axis=0
+        )
         turned = dot(parts_of(density.T, 1), right_ref[...], ((1,), (1,)))
         turned = slim_lines(turned)
         for j in range(lines):
@@ -184,80 +192,94 @@
                 u_ref[h, pl.ds(row, grid, stride=grid), :] = values[:, h * LANES : (h + 1) * LANES]
         return 0
 
-    def backward(d, c, _):
+    def backward(s, c, _):
         lanes = pl.ds(pl.multiple_of(c * step, step), step)
         values = jnp.concatenate([u_ref[h, lanes, :] for h in range(halves)], axis=1)
         values = slim_lines(values)
         potential = dot(right_ref[...], parts_of(values, 1), ((1,), (1,)))
-        visit = visit_ref[d, :, lanes].astype(jnp.float32)
-        total = None
-        for n in range(count):
-            one = potential[n * grid : (n + 1) * grid, :]
-            term = visit * one
-            if d > 0:
-                term = term + home_ref[n, :, lanes]
-            home_ref[n, :, lanes] = term
-            term = own_of(n, lanes) * one
-            total = term if total is None else total + term
-        back_ref[d, :, lanes] = total
+        visits = [visit_ref[d, :, lanes].astype(jnp.float32) for d in range(ROUNDS)]
+        totals = [back_ref[d, :, lanes] if s > 0 else None for d in range(ROUNDS)]
+        for n in range(per_set):
+            home = None
+            own = own_of(s * per_set + n, lanes)
+            for d in range(ROUNDS):
+                pair = n * ROUNDS + d
+                one = potential[pair * grid : (pair + 1) * grid, :]
+                home = visits[d] * one if home is None else home + visits[d] * one
+                totals[d] = own * one if totals[d] is None else totals[d] + own * one
+            home_ref[s * per_set + n, :, lanes] = home
+        for d in range(ROUNDS):
+            back_ref[d, :, lanes] = totals[d]
         return 0
 
     chunks = part // step
-    home_copies = [[] for _ in range(PARTS)]
+    sets = count // per_set
+    home_copies = [[[] for _ in range(PARTS)] for _ in range(sets)]
     back_copies = [[[] for _ in range(PARTS)] for _ in range(ROUNDS)]
     for copy in locals_:
         copy.wait()
-    for d in range(ROUNDS):
+    for s in range(sets):
         for p in range(PARTS):
-            arrivals[d][p].wait_recv()
-            lax.fori_loop(p * chunks, (p + 1) * chunks, functools.partial(forward, d), 0, unroll=UNROLL)
+            if s == 0:
+                for d in range(ROUNDS):
+                    arrivals[p][d].wait_recv()
+            lax.fori_loop(
+                p * chunks, (p + 1) * chunks, functools.partial(forward, s), 0, unroll=UNROLL
+            )
         lax.fori_loop(0, grid // lines, middle, 0, unroll=UNROLL)
         for p in range(PARTS):
-            lax.fori_loop(p * chunks, (p + 1) * chunks, functools.partial(backward, d), 0, unroll=UNROLL)
+            lax.fori_loop(
+                p * chunks, (p + 1) * chunks, functools.partial(backward, s), 0, unroll=UNROLL
+            )
             lanes = lanes_of(p)
-            for by in range(groups):
-                back_copies[d][p].append(
+            if s == sets - 1:
+                for d in range(ROUNDS):
+                    for by in range(groups):
+                        back_copies[d][p].append(
+                            remote(
+                                back_ref.at[d, rows_of(by), lanes],
+                                back_got.at[d, by, :, lanes],
+                                back_send.at[d, by, p],
+                                back_recv.at[d, by, p],
+                                device(by, -d - 1),
+                            )
+                        )
+            members = pl.ds(s * per_set, per_set)
+            for by in range(1, groups):
+                home_copies[s][p].append(
                     remote(
-                        back_ref.at[d, rows_of(by), lanes],
-                        back_got.at[d, by, :, lanes],
-                        back_send.at[d, by, p],
-                        back_recv.at[d, by, p],
-                        device(by, -d - 1),
+                        home_ref.at[members, rows_of(by), lanes],
+                        home_got.at[by - 1, members, :, lanes],
+                        home_send.at[by - 1, s, p],
+                        home_recv.at[by - 1, s, p],
+                        device(by, 0),
                     )
                 )
-            if d == ROUNDS - 1:
-                for by in range(1, groups):
-                    home_copies[p].append(
-                        remote(
-                            home_ref.at[:, rows_of(by), lanes],
-                            home_got.at[by - 1, :, :, lanes],
-                            home_send.at[by - 1, p],
-                            home_recv.at[by - 1, p],
-                            device(by, 0),
-                        )
-                    )
 
     if count < own_count:
         out_ref[...] = jnp.zeros_like(out_ref)
     out_ref[pl.ds(own_start, count)] = home_ref[:, rows_of(0), :]
-    for d in range(ROUNDS):
+    for s in range(sets):
         for p in range(PARTS):
             lanes = lanes_of(p)
-            if d == ROUNDS - 1:
-                for by in range(1, groups):
-                    home_copies[p][by - 1].wait_recv()
-                    source = lax.rem(group + groups - by, groups)
-                    start = lax.rem(source, split_count) * count
-                    out_ref[pl.ds(start, count), :, lanes] += home_got[by - 1, :, :, lanes]
-            for by in range(groups):
-                back_copies[d][p][by].wait_recv()
-                row = lax.rem(group + groups - by, groups) // split_count
-                out_ref[row, :, lanes] += back_got[d, by, :, lanes]
+            for by in range(1, groups):
+                home_copies[s][p][by - 1].wait_recv()
+                source = lax.rem(group + groups - by, groups)
+                start = lax.rem(source, split_count) * count + s * per_set
+                members = pl.ds(s * per_set, per_set)
+                out_ref[pl.ds(start, per_set), :, lanes] += home_got[by - 1, members, :, lanes]
+            if s == sets - 1:
+                for d in range(ROUNDS):
+                    for by in range(groups):
+                        back_copies[d][p][by].wait_recv()
+                        row = lax.rem(group + groups - by, groups) // split_count
+                        out_ref[row, :, lanes] += back_got[d, by, :, lanes]
     for p in range(PARTS):
-        for copy in home_copies[p]:
-            copy.wait_send()
+        for s in range(sets):
+            for copy in home_copies[s][p]:
+                copy.wait_send()
         for d in range(ROUNDS):
-            arrivals[d][p].wait_send()
+            arrivals[p][d].wait_send()
             for copy in back_copies[d][p]:
                 copy.wait_send()
 
@@ -267,12 +289,13 @@
     groups, ring = lax.axis_size("grp"), lax.axis_size("band")
     count = own_count // (groups // own_count)
     planes = grid // groups
-    width = count * grid
+    per_set = bands_per_set(count)
+    width = per_set * ROUNDS * grid
     step = 4 * grid
     table = kernel_table(grid).reshape(grid * grid, grid) * (-0.25 / float(grid**3))
     consts = (
         jnp.asarray(np.tile(table, (1, LANES // grid)).astype(np.float32)),
-        jnp.asarray(tables(grid, count)),
+        jnp.asarray(tables(grid, per_set * ROUNDS)),
         jnp.asarray(tables(grid, 1)),
     )
     vmem = pl.BlockSpec(memory_space=pltpu.VMEM)
@@ -280,7 +303,7 @@
     return pl.pallas_call(
         functools.partial(exchange_kernel, grid, step, groups, ring),
         out_shape=jax.ShapeDtypeStruct((own_count, planes, plane), jnp.float32),
-        in_specs=[pl.BlockSpec(memory_space=pl.ANY)] * 4,
+        in_specs=[pl.BlockSpec(memory_space=pltpu.HBM)] * 4,
         out_specs=vmem,
         scratch_shapes=[
             pltpu.VMEM((count, grid, plane), jnp.bfloat16),
@@ -295,13 +318,13 @@
             dma((4,)),
             dma((ROUNDS, PARTS)),
             dma((ROUNDS, PARTS)),
-            dma((groups - 1, PARTS)),
-            dma((groups - 1, PARTS)),
+            dma((groups - 1, count // per_set, PARTS)),
+            dma((groups - 1, count // per_set, PARTS)),
             dma((ROUNDS, groups, PARTS)),
             dma((ROUNDS, groups, PARTS)),
         ],
         compiler_params=pltpu.CompilerParams(
-            collective_id=0, has_side_effects=True, vmem_limit_bytes=48 * 1024 * 1024
+            collective_id=0, has_side_effects=True, vmem_limit_bytes=60 * 1024 * 1024
         ),
     )(orbitals, *consts)
 

time: 108 us -> 108 us (level)
  local copies, waits for them, and re-layouts: 5.91 us -> 2.27 us
  Pallas kernels: 102 us -> 105 us
    unnamed x9 -> x1, local copies, waits for them, and re-layouts: 5.91 us -> 2.27 us
    pallas_call x1, Pallas kernels: 102 us -> 105 us  [body(): pl.pallas_call(functools.partial(exchange_kernel, grid, step, groups, rin...]
where the time goes in v4:
time: 108 us; the launch traced here: 107 us
  Pallas kernels  105 us (97%)
  local copies, waits for them, and re-layouts  2.27 us (2%)
    pallas_call x1, Pallas kernels, body(): pl.pallas_call(functools.partial(exchange_kernel, grid, step, groups, rin...  105 us
    unnamed x1, local copies, waits for them, and re-layouts  2.27 us

profile of v4, /device:TPU:1, one launch (start us, length us, event | category | flops | bytes accessed | tf_op | source)
XLA Modules:
  0.0 107.4 jit_solution(11368775713248729482)
XLA Ops:
  0.0 105.1 %shard_map.46 = f32[4,16,4096]{2,1,0:T(8,128)} custom-call(bf16[4,64,4096]{2,1,0:T(8,128)(2,1)} %orbitals_ref.1, f32[4096,128]{1,0:T(8,128)} %constant.6.clone.table_hbm, bf16[256,768]{1,0:T(8,128)(2,1)} %constant.7.clone.right_hbm, bf16[64,192]{1,0:T(8,128)(2,1)} %constant.8.clone.slim_hbm), custom_call_target="tpu_custom_call" | custom-call | tf_op jit(solution)/shard_map/pallas_call | solution.py:303
  105.1 2.3 %copy.6 = f32[4,16,4096]{2,1,0:T(8,128)} copy(f32[4,16,4096]{2,1,0:T(8,128)} %shard_map.46) | data formatting | bytes 2097152

commit v5 on v3

--- a/solution.py
+++ b/solution.py
@@ -301,7 +301,7 @@
             dma((ROUNDS, groups, PARTS)),
         ],
         compiler_params=pltpu.CompilerParams(
-            collective_id=0, has_side_effects=True, vmem_limit_bytes=48 * 1024 * 1024
+            collective_id=0, has_side_effects=True, vmem_limit_bytes=60 * 1024 * 1024
         ),
     )(orbitals, *consts)
 

time: 108 us -> 105 us (0.972)
  local copies, waits for them, and re-layouts: 5.91 us -> 2.27 us
    unnamed x9 -> x1, local copies, waits for them, and re-layouts: 5.91 us -> 2.27 us
where the time goes in v5:
time: 105 us
  Pallas kernels  102 us (97%)
  local copies, waits for them, and re-layouts  2.27 us (2%)
    pallas_call x1, Pallas kernels, body(): pl.pallas_call(functools.partial(exchange_kernel, grid, step, groups, rin...  102 us
    unnamed x1, local copies, waits for them, and re-layouts  2.27 us

profile of v5, /device:TPU:1, one launch (start us, length us, event | category | flops | bytes accessed | tf_op | source)
XLA Modules:
  0.0 104.5 jit_solution(10611048520974923572)
XLA Ops:
  0.0 102.2 %shard_map.46 = f32[4,16,4096]{2,1,0:T(8,128)} custom-call(bf16[4,64,4096]{2,1,0:T(8,128)(2,1)} %orbitals_ref.1, f32[4096,128]{1,0:T(8,128)} %constant.6.clone.table_hbm, bf16[256,768]{1,0:T(8,128)(2,1)} %constant.7.clone.right_hbm, bf16[64,192]{1,0:T(8,128)(2,1)} %constant.8.clone.slim_hbm), custom_call_target="tpu_custom_call" | custom-call | tf_op jit(solution)/shard_map/pallas_call | solution.py:280
  102.3 2.3 %copy.6 = f32[4,16,4096]{2,1,0:T(8,128)} copy(f32[4,16,4096]{2,1,0:T(8,128)} %shard_map.46) | data formatting | bytes 2097152

commit v6 on v5

--- a/solution.py
+++ b/solution.py
@@ -60,6 +60,7 @@
     table_hbm,
     right_hbm,
     slim_hbm,
+    kept_ref,
     out_ref,
     own_ref,
     table_ref,
@@ -238,8 +239,9 @@
                     )
 
     if count < own_count:
-        out_ref[...] = jnp.zeros_like(out_ref)
-    out_ref[pl.ds(own_start, count)] = home_ref[:, rows_of(0), :]
+        kept_ref[...] = jnp.zeros_like(kept_ref)
+    kept_ref[pl.ds(own_start, count)] = home_ref[:, rows_of(0), :]
+    out_ref[...] = jnp.zeros_like(out_ref)
     for d in range(ROUNDS):
         for p in range(PARTS):
             lanes = lanes_of(p)
@@ -277,11 +279,11 @@
     )
     vmem = pl.BlockSpec(memory_space=pltpu.VMEM)
     dma = pltpu.SemaphoreType.DMA
-    return pl.pallas_call(
+    kept, received = pl.pallas_call(
         functools.partial(exchange_kernel, grid, step, groups, ring),
-        out_shape=jax.ShapeDtypeStruct((own_count, planes, plane), jnp.float32),
+        out_shape=(jax.ShapeDtypeStruct((own_count, planes, plane), jnp.float32),) * 2,
         in_specs=[pl.BlockSpec(memory_space=pl.ANY)] * 4,
-        out_specs=vmem,
+        out_specs=(vmem, vmem),
         scratch_shapes=[
             pltpu.VMEM((count, grid, plane), jnp.bfloat16),
             *[pltpu.VMEM(c.shape, c.dtype) for c in consts],
@@ -304,6 +306,7 @@
             collective_id=0, has_side_effects=True, vmem_limit_bytes=60 * 1024 * 1024
         ),
     )(orbitals, *consts)
+    return kept + received
 
 
 def solution(mesh):

time: 105 us -> 106 us (level)
  other arithmetic: 0 us -> 2.62 us
  local copies, waits for them, and re-layouts: 2.27 us -> 0 us
    add x0 -> x1, other arithmetic: none -> 2.62 us  [body(): return kept + received]
    unnamed x1 -> x0, local copies, waits for them, and re-layouts: 2.27 us -> none
where the time goes in v6:
time: 106 us; the launch traced here: 105 us
  Pallas kernels  103 us (97%)
  other arithmetic  2.62 us (2%)
    pallas_call x1, Pallas kernels, body(): pl.pallas_call(functools.partial(exchange_kernel, grid, step, groups, rin...  103 us
    add x1, other arithmetic, body(): return kept + received  2.62 us

profile of v6, /device:TPU:1, one launch (start us, length us, event | category | flops | bytes accessed | tf_op | source)
XLA Modules:
  0.0 105.2 jit_solution(12648970592400738567)
XLA Ops:
  0.0 102.6 %shard_map.46 = (f32[4,16,4096]{2,1,0:T(8,128)}, f32[4,16,4096]{2,1,0:T(8,128)}) custom-call(bf16[4,64,4096]{2,1,0:T(8,128)(2,1)} %orbitals_ref.1, f32[4096,128]{1,0:T(8,128)} %constant.6.clone.table_hbm, bf16[256,768]{1,0:T(8,128)(2,1)} %constant.7.clone.right_hbm, bf16[64,192]{1,0:T(8,128)(2,1)} %constant.8.clone.slim_hbm), custom_call_target="tpu_custom_call" | custom-call | tf_op jit(solution)/shard_map/pallas_call | solution.py:282
  102.6 2.6 %add.3 = f32[4,16,4096]{2,1,0:T(8,128)} add(f32[4,16,4096]{2,1,0:T(8,128)} %get-tuple-element.7, f32[4,16,4096]{2,1,0:T(8,128)} %get-tuple-element.8) | non-fusion elementwise | flops 262144 | bytes 3145728 | tf_op jit(solution)/shard_map/add | solution.py:309
